TPU v7x, 32 devices: a whole 2x2x4 slice. The times are simulated.
32 devices in a mesh: groups: 2 (over y), blk: 8 (over z, core), width: 2 (over x).
Axes of the slice: x: 2, y: 2, z: 4, core: 2. Of those that a mesh axis runs over, the one named last changes fastest.
Arguments:
- tokens: bfloat16 [448, 4096], P(('groups', 'blk'), 'width'), parts along dimension 0, may hold values from -6 to 6
- grad_hidden: bfloat16 [448, 28672], P('groups', 'blk'), parts along dimension 0, may hold values from -2 to 2
- codes: bfloat16 [2, 4096, 28672], P(None, 'width', 'blk'), may hold values from -8 to 7, as said below
- scales: float32 [2, 32, 28672], P(None, 'width', 'blk'), may hold values from 0.0015625 to 0.015625
- pattern: int32 [224, 32], P('blk', 'width'), may hold values from 0 to 1
Outputs:
- grad_tokens: bfloat16 [448, 4096], P(('groups', 'blk'), 'width'), parts along dimension 0
- grad_log_scales: float32 [2, 64, 28672], P(None, ('groups', 'width'), 'blk'), parts along dimension 1
There are 2 independent parts, one for each index of `groups`. A program takes and returns all parts, laid end to end along the dimension named above; an argument that names none is the same for every part. Nothing has to cross between parts.
Inputs may be any that keep to these rules, and one draw needn't show every extreme that they name: `codes`: every code is a whole number.
All inputs are finite; a program needn't handle non-finite values.
Results may differ from a plain program's by a relative error of at most 0.017.
Values may be sent and summed in bfloat16 or wider, within the bound.
A program may use at most 192 MiB of HBM per device.

v0:
```python
import jax
import jax.numpy as jnp
from jax import lax
from jax.sharding import PartitionSpec as P


def dequantize(codes, scales, pattern):
    rows_tile = scales.shape[1]
    block = codes.shape[1] // rows_tile
    cols = codes.shape[2]
    mask = jnp.repeat(pattern.T, block, axis=1).astype(jnp.float32)
    factor = scales * mask[None]
    values = codes.astype(jnp.float32).reshape(2, rows_tile, block, cols) * factor[:, :, None, :]
    weight = values.reshape(codes.shape).astype(jnp.bfloat16)
    return (jnp.concatenate((weight[0], weight[1]), axis=1), factor)


def back_gates(hidden, upstream):
    half = upstream.shape[1]
    gate = hidden[:, :half]
    up = hidden[:, half:]
    grad_in = upstream.astype(jnp.float32)
    sig = jax.nn.sigmoid(gate)
    grad_gate = grad_in * up * sig * (1.0 + gate * (1.0 - sig))
    grad_up = grad_in * gate * sig
    return jnp.concatenate((grad_gate, grad_up), axis=1).astype(jnp.bfloat16)


def on_device(tokens, grad_hidden, codes, scales, pattern):
    cols_tile, rows_tile = pattern.shape
    block = codes.shape[1] // rows_tile
    slice_f = codes.shape[2]
    gathered = lax.all_gather(tokens, "blk", axis=0, tiled=True)
    joined, factor = dequantize(codes, scales, pattern)
    hidden = lax.psum(
        jnp.dot(gathered, joined, preferred_element_type=jnp.float32).astype(jnp.bfloat16), "width"
    ).astype(jnp.float32)
    grads = back_gates(hidden, grad_hidden)
    grad_tokens = lax.psum_scatter(
        lax.dot_general(
            grads, joined, (((1,), (1,)), ((), ())), preferred_element_type=jnp.float32
        ).astype(jnp.bfloat16),
        "blk",
        scatter_dimension=0,
        tiled=True,
    )
    weight_grad = lax.dot_general(
        gathered, grads, (((0,), (0,)), ((), ())), preferred_element_type=jnp.float32
    )
    codes_joined = jnp.concatenate((codes[0], codes[1]), axis=1).astype(jnp.float32)
    summed = (weight_grad * codes_joined).reshape(rows_tile, block, 2 * slice_f).sum(axis=1)
    factor_joined = jnp.concatenate((factor[0], factor[1]), axis=1)
    return (grad_tokens, (summed * factor_joined).reshape(rows_tile, 2, slice_f).transpose(1, 0, 2))


def solution(mesh):
    return jax.shard_map(
        on_device,
        mesh=mesh,
        in_specs=(
            P(("groups", "blk"), "width"),
            P("groups", "blk"),
            P(None, "width", "blk"),
            P(None, "width", "blk"),
            P("blk", "width"),
        ),
        out_specs=(P(("groups", "blk"), "width"), P(None, ("groups", "width"), "blk")),
        check_vma=False,
    )
```

profile of v0, /device:TPU:0, one launch (start us, length us, event | category | flops | bytes accessed | tf_op | source)
XLA Modules:
  0.0 245.3 jit_solution(5949424410235880979)
XLA Ops:
  7.2 0.0 all-reduce.4.cloned.1.call-start
  7.2 0.7 convert_bitcast_fusion
  7.9 0.1 broadcast_in_dim.2
  8.0 0.1 copy.16
  8.2 1.5 copy_multiply_fusion
  9.7 0.1 copy.11
  9.8 20.5 %fusion.1 = bf16[2,2048,3584]{2,1,0:T(8,128)(2,1)} fusion(bf16[2,2048,3584]{2,1,0:T(8,128)(2,1)} %param.7, f32[2,16,3584]{2,1,0:T(8,128)S(1)} %copy.11), kind=kLoop, calls=%fused_computation.3 | loop fusion | flops 44040192 | bytes 59179008 | tf_op jit(solution)/shard_map/convert_element_type | solution.py:14
  30.3 0.0 copy-start.4
  30.3 21.6 %slice_bitcast_fusion.1 = (bf16[2048,3584]{1,0:T(8,128)(2,1)}, bf16[2048,3584]{1,0:T(8,128)(2,1)}) fusion(bf16[2,2048,3584]{2,1,0:T(8,128)(2,1)} %fusion.1), kind=kLoop, calls=%fused_computation.8 | loop fusion | bytes 58720256 | tf_op jit(solution)/shard_map/squeeze | solution.py:15
  51.9 0.0 copy-done.4
  51.9 18.3 %all-gather = bf16[8,28,2048]{2,1,0:T(8,128)(2,1)S(1)} all-gather(bf16[1,28,2048]{2,1,0:T(8,128)(2,1)S(1)} %bitcast.40), channel_id=1, replica_groups=mesh['groups'=2,'blk'=8,'width'=2] {'blk'}, dimensions={0}, use_global_device_ids=true | all-gather | bytes 1032192 | tf_op jit(solution)/shard_map/all_gather | solution.py:33
  70.2 0.2 reshape.26
  70.4 0.0 copy-start.2
  70.4 0.0 copy-start.5
  70.4 14.7 %fusion.5 = bf16[224,7168]{1,0:T(8,128)(2,1)} fusion(bf16[224,2048]{1,0:T(8,128)(2,1)S(1)} %reshape.26, bf16[2048,3584]{1,0:T(8,128)(2,1)} %get-tuple-element.9, bf16[2048,3584]{1,0:T(8,128)(2,1)} %get-tuple-element.8), kind=kOutput, calls=%fused_computation.12 | convolution fusion | flops 6636994560 | bytes 33488896 | tf_op jit(solution)/shard_map/dot_general | solution.py:36
  85.2 0.0 copy-done.2
  85.2 0.0 all-reduce.4.cloned.1.call-update
  85.2 1.1 slice_bitcast_fusion.5
  86.2 0.0 copy-done.5
  86.2 0.6 dynamic-slice.4
  87.5 21.6 %slice_bitcast_fusion.3 = (bf16[2048,3584]{1,0:T(8,128)(2,1)}, bf16[2048,3584]{1,0:T(8,128)(2,1)}) fusion(bf16[2,2048,3584]{2,1,0:T(8,128)(2,1)} %param.7), kind=kLoop, calls=%fused_computation.10 | loop fusion | bytes 58720256 | tf_op jit(solution)/shard_map/squeeze | solution.py:50
  109.1 0.0 copy-start
  109.1 65.0 %all-reduce.4.cloned.1.call-done = bf16[224,7168]{1,0:T(8,128)(2,1)} async-done(((bf16[224,7168]{1,0:T(8,128)(2,1)}), bf16[224,7168]{1,0:T(8,128)(2,1)}) %all-reduce.4.cloned.1.call-update) | async-done | bytes 3211280 | tf_op jit(solution)/shard_map/psum | solution.py:35
  174.0 2.6 %convert_element_type.47 = f32[224,7168]{1,0:T(8,128)S(1)} convert(bf16[224,7168]{1,0:T(8,128)(2,1)} %all-reduce.4.cloned.1.call-done) | non-fusion elementwise | flops 1605632 | bytes 9633792 | tf_op jit(solution)/shard_map/convert_element_type | solution.py:37
  176.6 0.0 copy-done
  176.7 1.6 fusion.8
  178.2 0.0 copy-start.1
  178.2 1.1 copy-done.1
  179.4 0.0 copy-start.3
  179.4 14.2 %fusion.11 = bf16[224,2048]{1,0:T(8,128)(2,1)} fusion(bf16[2048,3584]{1,0:T(8,128)(2,1)} %get-tuple-element.9, bf16[2048,3584]{1,0:T(8,128)(2,1)} %get-tuple-element.8, bf16[224,3584]{1,0:T(8,128)(2,1)S(1)} %get-tuple-element.11, bf16[224,3584]{1,0:T(8,128)(2,1)S(1)} %get-tuple-element.10), kind=kOutput, calls=%fused_computation.22 | convolution fusion | flops 6642270208 | bytes 33488896 | tf_op jit(solution)/shard_map/dot_general | solution.py:40
  193.6 22.4 %fusion = bf16[32,2048]{1,0:T(8,128)(2,1)S(1)} fusion(bf16[224,2048]{1,0:T(8,128)(2,1)} %fusion.11), kind=kCustom, calls=%all-reduce-scatter | all-reduce-scatter fusion | flops 524289 | bytes 1049088
  216.0 0.7 slice.38
  216.7 1.9 collective-permute-start
  218.7 0.0 copy-done.3
  218.7 14.2 %bitcast_reduce_fusion = f32[16,7168]{1,0:T(8,128)} fusion(bf16[224,2048]{1,0:T(8,128)(2,1)S(1)} %copy-done.3, bf16[2048,3584]{1,0:T(8,128)(2,1)} %get-tuple-element.7, bf16[2048,3584]{1,0:T(8,128)(2,1)} %get-tuple-element.6, bf16[224,3584]{1,0:T(8,128)(2,1)} %copy-done.1, bf16[224,3584]{1,0:T(8,128)(2,1)S(1)} %get-tuple-element.10), kind=kOutput, calls=%fused_computation | convolution fusion | flops 6671056896 | bytes 33947648 | tf_op jit(solution)/shard_map/dot_general | solution.py:47
  232.9 1.4 reduce_sum.12
  234.3 1.4 fusion.12
  235.8 0.9 copy.12
  236.6 0.0 collective-permute-done
  236.6 1.2 concatenate.24
  237.8 0.7 constant_dynamic-slice_fusion
Async XLA Ops:
  7.2 166.8 %all-reduce.4.cloned.1.call-start = ((), (), s32[]{:S(2)}) async-start(), calls=%async_computation | async-start | bytes 6422528 | tf_op jit(solution)/shard_map/psum | solution.py:35
  30.3 21.6 %copy-start.4 = (bf16[28,2048]{1,0:T(8,128)(2,1)S(1)}, bf16[28,2048]{1,0:T(8,128)(2,1)}, u32[]{:S(2)}) copy-start(bf16[28,2048]{1,0:T(8,128)(2,1)} %param.5) | copy-start | bytes 344068
  70.4 14.8 %copy-start.2 = (bf16[224,2048]{1,0:T(8,128)(2,1)}, bf16[224,2048]{1,0:T(8,128)(2,1)S(1)}, u32[]{:S(2)}) copy-start(bf16[224,2048]{1,0:T(8,128)(2,1)S(1)} %reshape.26) | copy-start | bytes 2752516
  70.4 15.8 %copy-start.5 = (u32[32]{0:T(128)S(1)}, u32[32]{0:T(128)}, u32[]{:S(2)}) copy-start(u32[32]{0:T(128)} %constant.8) | copy-start | bytes 388
  109.1 67.6 %copy-start = (bf16[224,3584]{1,0:T(8,128)(2,1)S(1)}, bf16[224,3584]{1,0:T(8,128)(2,1)}, u32[]{:S(2)}) copy-start(bf16[224,3584]{1,0:T(8,128)(2,1)} %param.6) | copy-start | bytes 4816900
  178.2 1.2 copy-start.1
  179.4 39.3 %copy-start.3 = (bf16[224,2048]{1,0:T(8,128)(2,1)S(1)}, bf16[224,2048]{1,0:T(8,128)(2,1)}, u32[]{:S(2)}) copy-start(bf16[224,2048]{1,0:T(8,128)(2,1)} %copy-done.2) | copy-start | bytes 2752516
  216.7 19.9 %collective-permute-start = (bf16[28,2048]{1,0:T(8,128)(2,1)}, bf16[28,2048]{1,0:T(8,128)(2,1)}, u32[]{:S(2)}, u32[]{:S(2)}) collective-permute-start(bf16[28,2048]{1,0:T(8,128)(2,1)} %slice.38), channel_id=1, source_target_pairs={{0,2},{2,4},{4,6},{6,8},{8,10},{10,12},{12,14},{1,3},{3,5},{5,7},{... | collective-permute-start | bytes 344072
Sparse Core Ops, SparseCore 0:
  85.3 88.6 all-reduce.3
where the time goes:
time: 246 us; the launch traced here: 245 us
  waiting for transfers between devices  65 us (26%)
  local copies, waits for them, and re-layouts  51.3 us (21%)
  matrix products  43.2 us (18%)
  blocking collectives  40.8 us (17%)
  other arithmetic  28.4 us (12%)
  between operations  14.8 us (6%)
    psum x1, waiting for transfers between devices, on_device(): lax.psum(jnp.dot(gathered, joined, preferred_element_type=jnp.float32).as...  65 us
    unnamed x1, blocking collectives  22.4 us
    squeeze x1, local copies, waits for them, and re-layouts, on_device(): codes[0]  21.6 us
    squeeze x1, local copies, waits for them, and re-layouts, dequantize(): return (jnp.concatenate((weight[0], weight[1]), axis=1), factor)  21.6 us
    convert_element_type x1, other arithmetic, dequantize(): weight = values.reshape(codes.shape).astype(jnp.bfloat16)  20.5 us
    all_gather x1, blocking collectives, on_device(): gathered = lax.all_gather(tokens, 'blk', axis=0, tiled=True)  18.3 us
    dot_general x1, matrix products, on_device(): jnp.dot(gathered, joined, preferred_element_type=jnp.float32)  14.7 us
    dot_general x1, matrix products, on_device(): lax.dot_general(gathered, grads, (((0,), (0,)), ((), ())), preferred_elem...  14.2 us
  transfers between devices with their start and end apart: 2, of which 1 were waited for; matrix products, arithmetic and copies ran while one was open for 17% of the time, Pallas kernels for 0%

commit v1 on v0

--- a/solution.py
+++ b/solution.py
@@ -1,6 +1,8 @@
 import jax
 import jax.numpy as jnp
 from jax import lax
+from jax.experimental import pallas as pl
+from jax.experimental.pallas import tpu as pltpu
 from jax.sharding import PartitionSpec as P
 
 
@@ -53,9 +55,308 @@
     return (grad_tokens, (summed * factor_joined).reshape(rows_tile, 2, slice_f).transpose(1, 0, 2))
 
 
+FC = 256
+AHEAD = 4
+FIRST = 6
+PAD = 32
+
+
+def dot(a, b, dims=((1,), (0,))):
+    return lax.dot_general(a, b, (dims, ((), ())), preferred_element_type=jnp.float32)
+
+
+def kernel(
+    tokens_ref, hidden_ref, codes_ref, scales_ref, pattern_ref, out_ref, gls_ref,
+    w_ref, mine_ref, theirs_ref, gath_ref, tok_ref, tokt_ref, gh_ref, acc_ref,
+    far_out, sib_in, far_sum, far_in, near_out, near_in,
+    codes_sem, gh_sem, xs_sem, xr_sem, ags_sem, agr_sem, sibs_sem, sibr_sem,
+    fars_sem, farr_sem, nears_sem, nearr_sem,
+):
+    chunks, _, depth, _ = w_ref.shape
+    items = 2 * chunks
+    rows = tok_ref.shape[1]
+    own_rows = tokens_ref.shape[0]
+    groups = scales_ref.shape[1]
+    block = depth // groups
+    blk = lax.axis_index("blk")
+    wide = lax.axis_index("width")
+    half = blk // 4
+    place = lax.rem(blk, 4)
+    core = lax.rem(blk, 2)
+    zlow = place // 2
+
+    def peer(rel):
+        bit0 = core if rel % 2 == 0 else 1 - core
+        bit1 = zlow if (rel // 2) % 2 == 0 else 1 - zlow
+        bit2 = half if rel // 4 == 0 else 1 - half
+        return bit2 * 4 + bit1 * 2 + bit0
+
+    def remote(src, dst, send, recv, target):
+        return pltpu.make_async_remote_copy(
+            src_ref=src, dst_ref=dst, send_sem=send, recv_sem=recv,
+            device_id=target, device_id_type=pl.DeviceIdType.MESH,
+        )
+
+    def codes_copy(c):
+        return pltpu.make_async_copy(
+            codes_ref.at[:, :, pl.ds(pl.multiple_of(c * FC, FC), FC)], w_ref.at[c], codes_sem.at[c]
+        )
+
+    def gh_copy(g):
+        which = half if g == 0 else 1 - half
+        return pltpu.make_async_copy(
+            hidden_ref.at[pl.ds(pl.multiple_of(which * rows, 16), rows)], gh_ref.at[g], gh_sem.at[g]
+        )
+
+    def ag_copy(rel):
+        if rel in (1, 2, 4, 6):
+            return remote(gath_ref.at[0], gath_ref.at[rel], ags_sem.at[rel], agr_sem.at[rel], {"blk": peer(rel)})
+        return remote(gath_ref.at[rel - 1], gath_ref.at[rel], ags_sem.at[rel], agr_sem.at[rel], {"blk": peer(1)})
+
+    def x_copy(i):
+        return remote(mine_ref.at[i], theirs_ref.at[i], xs_sem.at[i], xr_sem.at[i], {"width": 1 - wide})
+
+    def sib_copy(z):
+        return remote(far_out.at[2 * z + 1 - core], sib_in.at[z], sibs_sem.at[z], sibr_sem.at[z], {"blk": peer(1)})
+
+    def far_copy(z):
+        target = (1 - half) * 4 + z * 2 + core
+        return remote(far_sum.at[z], far_in.at[zlow], fars_sem.at[z], farr_sem.at[zlow], {"blk": target})
+
+    def near_copy(rel):
+        j = lax.rem(peer(rel), 4)
+        return remote(near_out.at[j], near_in.at[rel - 1], nears_sem.at[rel - 1], nearr_sem.at[rel - 1], {"blk": peer(rel)})
+
+    lax.fori_loop(0, chunks, lambda c, _: (codes_copy(c).start(), 0)[1], 0)
+    for g in range(2):
+        gh_copy(g).start()
+
+    barrier = pltpu.get_barrier_semaphore()
+    pl.semaphore_signal(barrier, inc=1, device_id={"width": 1 - wide}, device_id_type=pl.DeviceIdType.MESH)
+    for rel in (1, 2, 3, 4, 6):
+        pl.semaphore_signal(barrier, inc=1, device_id={"blk": peer(rel)}, device_id_type=pl.DeviceIdType.MESH)
+    gath_ref[0] = jnp.concatenate(
+        [tokens_ref[...], jnp.zeros((PAD - own_rows, depth), tokens_ref.dtype)], axis=0
+    )
+    acc_ref[...] = jnp.zeros_like(acc_ref)
+    pl.semaphore_wait(barrier, 6)
+    for rel in (2, 1, 6, 4):
+        ag_copy(rel).start()
+
+    def select(shape, dim):
+        short = lax.broadcasted_iota(jnp.int32, shape, dim)
+        long = lax.broadcasted_iota(jnp.int32, shape, 1 - dim)
+        slot = long >> 5
+        hit = (long - 4 * slot == short) & (long - 32 * slot < own_rows)
+        return jnp.where(hit, 1.0, 0.0).astype(jnp.bfloat16)
+
+    def compact(g):
+        pick = select((rows, 4 * PAD), 0)
+        joined = []
+        for j in range(4):
+            jz, jc = j // 2, j % 2
+            dz = jnp.where(zlow == jz, 0, 1)
+            dc = jnp.where(core == jc, 0, 1)
+            joined.append(gath_ref[4 * g + 2 * dz + dc])
+        tok_ref[g] = dot(pick, jnp.concatenate(joined, axis=0)).astype(jnp.bfloat16)
+
+    def spread(g):
+        pick = select((4 * PAD, rows), 1)
+        return dot(pick, acc_ref[g].astype(jnp.bfloat16)).astype(jnp.bfloat16).reshape(4, PAD, depth)
+
+    ag_copy(2).wait_recv()
+    ag_copy(3).start()
+    ag_copy(1).wait_recv()
+    ag_copy(3).wait_recv()
+    compact(0)
+    for g in range(2):
+        gh_copy(g).wait()
+
+    def place_of(i):
+        first = i < FIRST
+        other = (i >= FIRST) & (i < FIRST + chunks)
+        g = jnp.where(other, 1, 0)
+        c = jnp.where(first, i, jnp.where(other, i - FIRST, i - chunks))
+        return g, c
+
+    def prepare(c):
+        codes_copy(c).wait()
+        cols = pl.ds(pl.multiple_of(c * FC, FC), FC)
+        lane = lax.broadcasted_iota(jnp.int32, (1, FC), 1)
+
+        def body(r, _):
+            left = pattern_ref[2 * c, r].astype(jnp.float32)
+            right = pattern_ref[2 * c + 1, r].astype(jnp.float32)
+            kept = jnp.where(lane < block, left, right)
+            rowsel = pl.ds(pl.multiple_of(r * block, block), block)
+            for m in range(2):
+                factor = scales_ref[m, pl.ds(r, 1), cols] * kept
+                w_ref[c, m, rowsel, :] = (
+                    w_ref[c, m, rowsel, :].astype(jnp.float32) * factor
+                ).astype(jnp.bfloat16)
+            return 0
+
+        lax.fori_loop(0, groups, body, 0)
+
+    def forward(i):
+        g, c = place_of(i)
+        pl.when((i < FIRST) | ((g == 1) & (c >= FIRST)))(lambda: prepare(c))
+        for m in range(2):
+            mine_ref[i, m] = dot(tok_ref[g], w_ref[c, m]).astype(jnp.bfloat16)
+        x_copy(i).start()
+
+    def backward(i):
+        g, c = place_of(i)
+        x_copy(i).wait_recv()
+        cols = pl.ds(pl.multiple_of(c * FC, FC), FC)
+        gate = mine_ref[i, 0].astype(jnp.float32) + theirs_ref[i, 0].astype(jnp.float32)
+        up = mine_ref[i, 1].astype(jnp.float32) + theirs_ref[i, 1].astype(jnp.float32)
+        grad_in = gh_ref[g, :, cols].astype(jnp.float32)
+        sig = jax.nn.sigmoid(gate)
+        theirs_ref[i, 0] = (grad_in * up * sig * (1.0 + gate * (1.0 - sig))).astype(jnp.bfloat16)
+        theirs_ref[i, 1] = (grad_in * gate * sig).astype(jnp.bfloat16)
+        both = dot(theirs_ref[i, 0], w_ref[c, 0], ((1,), (1,)))
+        acc_ref[g] += both + dot(theirs_ref[i, 1], w_ref[c, 1], ((1,), (1,)))
+
+        @pl.when((i >= FIRST) & (i < 2 * FIRST) | (i >= FIRST + chunks))
+        def _():
+            own = jnp.where(i < 2 * FIRST, i - FIRST, i)
+            far = jnp.where(i < 2 * FIRST, i, i - chunks + FIRST)
+            for m in range(2):
+                grads = jnp.concatenate([theirs_ref[own, m], theirs_ref[far, m]], axis=0)
+                for q in range(4):
+                    part = depth // 4
+                    wg = dot(tokt_ref[q * part : (q + 1) * part, :], grads)
+                    prod = wg * w_ref[c, m, q * part : (q + 1) * part, :].astype(jnp.float32)
+                    gls_ref[m, q * (groups // 4) : (q + 1) * (groups // 4), cols] = (
+                        prod.reshape(groups // 4, block, FC).sum(axis=1)
+                    )
+
+    def second_half():
+        for rel in (5, 7):
+            ag_copy(rel).wait_recv()
+        compact(1)
+        eye_r = lax.broadcasted_iota(jnp.int32, (FC, FC), 0)
+        eye_c = lax.broadcasted_iota(jnp.int32, (FC, FC), 1)
+        eye = jnp.where(eye_r == eye_c, 1.0, 0.0).astype(jnp.bfloat16)
+        for q in range(depth // FC):
+            sub = slice(q * FC, (q + 1) * FC)
+            whole = jnp.concatenate([tok_ref[0, :, sub], tok_ref[1, :, sub]], axis=0)
+            tokt_ref[sub, :] = dot(eye, whole, ((1,), (1,))).astype(jnp.bfloat16)
+
+    def hand_on():
+        for rel in (4, 6):
+            ag_copy(rel).wait_recv()
+            ag_copy(rel + 1).start()
+
+    def far_start():
+        far_out[...] = spread(1)
+        for z in range(2):
+            sib_copy(z).start()
+
+    def far_finish():
+        for z in range(2):
+            sib_copy(z).wait_recv()
+            far_sum[z] = (
+                far_out[2 * z + core].astype(jnp.float32) + sib_in[z].astype(jnp.float32)
+            ).astype(jnp.bfloat16)
+            far_copy(z).start()
+
+    def step(s, _):
+        pl.when(s == FIRST - 2)(hand_on)
+        pl.when(s == FIRST)(second_half)
+        pl.when(s < items)(lambda: forward(s))
+        pl.when(s >= AHEAD)(lambda: backward(s - AHEAD))
+        pl.when(s == FIRST + chunks + AHEAD - 1)(far_start)
+        pl.when(s == FIRST + chunks + AHEAD)(far_finish)
+        return 0
+
+    lax.fori_loop(0, items + AHEAD, step, 0)
+    near_out[...] = spread(0)
+    for rel in (3, 2, 1):
+        near_copy(rel).start()
+    total = near_out[place].astype(jnp.float32)
+    for z in range(2):
+        remote(far_sum.at[z], far_in.at[z], fars_sem.at[z], farr_sem.at[z], {"blk": peer(4)}).wait_recv()
+        total = total + far_in[z].astype(jnp.float32)
+    for rel in (1, 2, 3):
+        near_copy(rel).wait_recv()
+        total = total + near_in[rel - 1].astype(jnp.float32)
+    out_ref[...] = total[:own_rows].astype(out_ref.dtype)
+
+    for rel in (1, 2, 3, 4, 5, 6, 7):
+        ag_copy(rel).wait_send()
+    lax.fori_loop(0, items, lambda i, _: (x_copy(i).wait_send(), 0)[1], 0)
+    for z in range(2):
+        sib_copy(z).wait_send()
+        far_copy(z).wait_send()
+    for rel in (1, 2, 3):
+        near_copy(rel).wait_send()
+
+
+def fused(tokens, grad_hidden, codes, scales, pattern):
+    own_rows, depth = tokens.shape
+    slice_f = codes.shape[2]
+    chunks = slice_f // FC
+    items = 2 * chunks
+    rows = 4 * own_rows
+    bf16 = jnp.bfloat16
+    vmem = pl.BlockSpec(memory_space=pltpu.VMEM)
+    hbm = pl.BlockSpec(memory_space=pl.ANY)
+    dma = pltpu.SemaphoreType.DMA
+    return pl.pallas_call(
+        kernel,
+        out_shape=(
+            jax.ShapeDtypeStruct((own_rows, depth), bf16),
+            jax.ShapeDtypeStruct(scales.shape, jnp.float32),
+        ),
+        in_specs=[vmem, hbm, hbm, vmem, pl.BlockSpec(memory_space=pltpu.SMEM)],
+        out_specs=(vmem, vmem),
+        scratch_shapes=[
+            pltpu.VMEM((chunks, 2, depth, FC), bf16),
+            pltpu.VMEM((items, 2, rows, FC), bf16),
+            pltpu.VMEM((items, 2, rows, FC), bf16),
+            pltpu.VMEM((8, PAD, depth), bf16),
+            pltpu.VMEM((2, rows, depth), bf16),
+            pltpu.VMEM((depth, 2 * rows), bf16),
+            pltpu.VMEM((2, rows, slice_f), bf16),
+            pltpu.VMEM((2, rows, depth), jnp.float32),
+            pltpu.VMEM((4, PAD, depth), bf16),
+            pltpu.VMEM((2, PAD, depth), bf16),
+            pltpu.VMEM((2, PAD, depth), bf16),
+            pltpu.VMEM((2, PAD, depth), bf16),
+            pltpu.VMEM((4, PAD, depth), bf16),
+            pltpu.VMEM((3, PAD, depth), bf16),
+            dma((chunks,)), dma((2,)), dma((items,)), dma((items,)), dma((8,)), dma((8,)),
+            dma((2,)), dma((2,)), dma((2,)), dma((2,)), dma((3,)), dma((3,)),
+        ],
+        compiler_params=pltpu.CompilerParams(
+            collective_id=0, has_side_effects=True, vmem_limit_bytes=60 * 1024 * 1024
+        ),
+        cost_estimate=pl.CostEstimate(
+            flops=6 * 2 * own_rows * 8 * depth * 2 * slice_f // 2,
+            bytes_accessed=codes.size * 2, transcendentals=0,
+        ),
+    )(tokens, grad_hidden, codes, scales, pattern)
+
+
+def device_program(mesh):
+    def run(tokens, grad_hidden, codes, scales, pattern):
+        fits = (
+            mesh.shape["blk"] == 8
+            and mesh.shape["width"] == 2
+            and tokens.shape[0] == 28
+            and codes.shape[1:] == (2048, 3584)
+        )
+        call = fused if fits else on_device
+        return call(tokens, grad_hidden, codes, scales, pattern)
+
+    return run
+
+
 def solution(mesh):
     return jax.shard_map(
-        on_device,
+        device_program(mesh),
         mesh=mesh,
         in_specs=(
             P(("groups", "blk"), "width"),

time: 246 us -> 102 us (0.41)
  Pallas kernels: 0 us -> 96.4 us
  waiting for transfers between devices: 65 us -> 0 us
  local copies, waits for them, and re-layouts: 51.3 us -> 4.77 us
  matrix products: 43.2 us -> 0 us
  blocking collectives: 40.8 us -> 0 us
  other arithmetic: 28.4 us -> 0 us
  between operations: 14.8 us -> 0.64 us
    pallas_call x0 -> x1, Pallas kernels: none -> 96.4 us  [fused(): pl.pallas_call(kernel, out_shape=(jax.ShapeDtypeStruct((own_rows, depth),...]
    psum x1 -> x0, waiting for transfers between devices: 65 us -> none  [on_device(): lax.psum(jnp.dot(gathered, joined, preferred_element_type=jnp.float32).as...]
    dot_general x3 -> x0, matrix products: 43.2 us -> none  [the longest x1 14.7 us: on_device(): jnp.dot(gathered, joined, preferred_element_type=jnp.float32)]
    squeeze x2 -> x0, local copies, waits for them, and re-layouts: 43.1 us -> none  [the longest x1 21.6 us: on_device(): codes[0]]
    convert_element_type x3 -> x0, other arithmetic: 23.9 us -> none  [the longest x1 20.5 us: dequantize(): weight = values.reshape(codes.shape).astype(jnp.bfloat16)]
    unnamed x1 -> x0, blocking collectives: 22.4 us -> none
    all_gather x1 -> x0, blocking collectives: 18.3 us -> none  [on_device(): gathered = lax.all_gather(tokens, 'blk', axis=0, tiled=True)]
    unnamed x19 -> x3, local copies, waits for them, and re-layouts: 5.47 us -> 4.77 us
  transfers between devices with their start and end apart: 2 -> 0, of which waited for: 1 -> 0; matrix products, arithmetic and copies ran while one was open for 17% -> 0% of each run, Pallas kernels for 0% -> 0%
where the time goes in v1:
time: 102 us
  Pallas kernels  96.4 us (95%)
  local copies, waits for them, and re-layouts  4.77 us (5%)
    pallas_call x1, Pallas kernels, fused(): pl.pallas_call(kernel, out_shape=(jax.ShapeDtypeStruct((own_rows, depth),...  96.4 us
    unnamed x3, local copies, waits for them, and re-layouts  4.77 us

profile of v1, /device:TPU:0, one launch (start us, length us, event | category | flops | bytes accessed | tf_op | source)
XLA Modules:
  0.0 101.9 jit_solution(7742197325530553333)
XLA Ops:
  0.6 1.4 %copy.7.pattern_ref = s32[28,16]{1,0:T(8,128)} copy(s32[28,16]{0,1:T(8,128)} %param.9) | data formatting | bytes 3584 | tf_op args[4]
  2.0 96.4 %shard_map.68 = (bf16[28,2048]{1,0:T(8,128)(2,1)}, f32[2,16,3584]{2,1,0:T(8,128)}) custom-call(bf16[28,2048]{1,0:T(8,128)(2,1)} %tokens_ref.1, bf16[224,3584]{1,0:T(8,128)(2,1)} %hidden_ref.1, bf16[2,2048,3584]{2,1,0:T(8,128)(2,1)} %codes_ref.1, f32[2,16,3584]{2,1,0:T(8,128)} %scales_ref.1, s32[28,16]{1,0:T(8,128)} %copy.7.pattern_ref), custom_call_target="tpu_custom_call" | custom-call | flops 19730006016 | bytes 29360128 | tf_op jit(solution)/shard_map/pallas_call | solution.py:307
  98.5 1.6 %copy.10 = bf16[28,2048]{1,0:T(8,128)(2,1)} copy(bf16[28,2048]{1,0:T(8,128)(2,1)} %get-tuple-element.4) | data formatting | bytes 229376
  100.0 1.8 %copy.11 = f32[2,16,3584]{2,1,0:T(8,128)} copy(f32[2,16,3584]{2,1,0:T(8,128)} %get-tuple-element.5) | data formatting | bytes 917504

commit v2 on v1

--- a/solution.py
+++ b/solution.py
@@ -57,7 +57,8 @@
 
 FC = 256
 AHEAD = 4
-FIRST = 6
+FETCH = 3
+FIRST = 8
 PAD = 32
 
 
@@ -68,7 +69,7 @@
 def kernel(
     tokens_ref, hidden_ref, codes_ref, scales_ref, pattern_ref, out_ref, gls_ref,
     w_ref, mine_ref, theirs_ref, gath_ref, tok_ref, tokt_ref, gh_ref, acc_ref,
-    far_out, sib_in, far_sum, far_in, near_out, near_in,
+    far_out, sib_in, far_sum, far_in, near_out, near_in, factor_ref,
     codes_sem, gh_sem, xs_sem, xr_sem, ags_sem, agr_sem, sibs_sem, sibr_sem,
     fars_sem, farr_sem, nears_sem, nearr_sem,
 ):
@@ -127,7 +128,7 @@
         j = lax.rem(peer(rel), 4)
         return remote(near_out.at[j], near_in.at[rel - 1], nears_sem.at[rel - 1], nearr_sem.at[rel - 1], {"blk": peer(rel)})
 
-    lax.fori_loop(0, chunks, lambda c, _: (codes_copy(c).start(), 0)[1], 0)
+    lax.fori_loop(0, FETCH, lambda c, _: (codes_copy(c).start(), 0)[1], 0)
     for g in range(2):
         gh_copy(g).start()
 
@@ -138,9 +139,8 @@
     gath_ref[0] = jnp.concatenate(
         [tokens_ref[...], jnp.zeros((PAD - own_rows, depth), tokens_ref.dtype)], axis=0
     )
-    acc_ref[...] = jnp.zeros_like(acc_ref)
     pl.semaphore_wait(barrier, 6)
-    for rel in (2, 1, 6, 4):
+    for rel in (2, 1):
         ag_copy(rel).start()
 
     def select(shape, dim):
@@ -164,8 +164,18 @@
         pick = select((4 * PAD, rows), 1)
         return dot(pick, acc_ref[g].astype(jnp.bfloat16)).astype(jnp.bfloat16).reshape(4, PAD, depth)
 
+    acc_ref[...] = jnp.zeros_like(acc_ref)
+    kept_blocks = pattern_ref[...].astype(jnp.float32).astype(jnp.bfloat16)
+    column = lax.broadcasted_iota(jnp.int32, (pattern_ref.shape[0], scales_ref.shape[2]), 1)
+    which = lax.broadcasted_iota(jnp.int32, column.shape, 0)
+    inside = (column >= which * block) & (column < (which + 1) * block)
+    mask = dot(kept_blocks, jnp.where(inside, 1.0, 0.0).astype(jnp.bfloat16), ((0,), (0,)))
+    for m in range(2):
+        factor_ref[m] = scales_ref[m] * mask
     ag_copy(2).wait_recv()
     ag_copy(3).start()
+    for rel in (6, 4):
+        ag_copy(rel).start()
     ag_copy(1).wait_recv()
     ag_copy(3).wait_recv()
     compact(0)
@@ -181,16 +191,13 @@
 
     def prepare(c):
         codes_copy(c).wait()
+        pl.when(c + FETCH < chunks)(lambda: codes_copy(c + FETCH).start())
         cols = pl.ds(pl.multiple_of(c * FC, FC), FC)
-        lane = lax.broadcasted_iota(jnp.int32, (1, FC), 1)
 
         def body(r, _):
-            left = pattern_ref[2 * c, r].astype(jnp.float32)
-            right = pattern_ref[2 * c + 1, r].astype(jnp.float32)
-            kept = jnp.where(lane < block, left, right)
             rowsel = pl.ds(pl.multiple_of(r * block, block), block)
             for m in range(2):
-                factor = scales_ref[m, pl.ds(r, 1), cols] * kept
+                factor = factor_ref[m, pl.ds(r, 1), cols]
                 w_ref[c, m, rowsel, :] = (
                     w_ref[c, m, rowsel, :].astype(jnp.float32) * factor
                 ).astype(jnp.bfloat16)
@@ -217,20 +224,23 @@
         theirs_ref[i, 1] = (grad_in * gate * sig).astype(jnp.bfloat16)
         both = dot(theirs_ref[i, 0], w_ref[c, 0], ((1,), (1,)))
         acc_ref[g] += both + dot(theirs_ref[i, 1], w_ref[c, 1], ((1,), (1,)))
-
-        @pl.when((i >= FIRST) & (i < 2 * FIRST) | (i >= FIRST + chunks))
-        def _():
-            own = jnp.where(i < 2 * FIRST, i - FIRST, i)
-            far = jnp.where(i < 2 * FIRST, i, i - chunks + FIRST)
-            for m in range(2):
-                grads = jnp.concatenate([theirs_ref[own, m], theirs_ref[far, m]], axis=0)
-                for q in range(4):
-                    part = depth // 4
-                    wg = dot(tokt_ref[q * part : (q + 1) * part, :], grads)
-                    prod = wg * w_ref[c, m, q * part : (q + 1) * part, :].astype(jnp.float32)
-                    gls_ref[m, q * (groups // 4) : (q + 1) * (groups // 4), cols] = (
-                        prod.reshape(groups // 4, block, FC).sum(axis=1)
-                    )
+        complete = (i >= FIRST) & (i < 2 * FIRST) | (i >= FIRST + chunks)
+        pl.when(complete & (i < items - 1))(lambda: step_grads(i))
+
+    def step_grads(i):
+        _, c = place_of(i)
+        cols = pl.ds(pl.multiple_of(c * FC, FC), FC)
+        own = jnp.where(i < 2 * FIRST, i - FIRST, i)
+        far = jnp.where(i < 2 * FIRST, i, i - chunks + FIRST)
+        for m in range(2):
+            grads = jnp.concatenate([theirs_ref[own, m], theirs_ref[far, m]], axis=0)
+            for q in range(4):
+                part = depth // 4
+                wg = dot(tokt_ref[q * part : (q + 1) * part, :], grads)
+                prod = wg * w_ref[c, m, q * part : (q + 1) * part, :].astype(jnp.float32)
+                gls_ref[m, q * (groups // 4) : (q + 1) * (groups // 4), cols] = (
+                    prod.reshape(groups // 4, block, FC).sum(axis=1)
+                )
 
     def second_half():
         for rel in (5, 7):
@@ -275,6 +285,7 @@
     near_out[...] = spread(0)
     for rel in (3, 2, 1):
         near_copy(rel).start()
+    lax.fori_loop(items - 1, items, lambda i, _: (step_grads(i), 0)[1], 0)
     total = near_out[place].astype(jnp.float32)
     for z in range(2):
         remote(far_sum.at[z], far_in.at[z], fars_sem.at[z], farr_sem.at[z], {"blk": peer(4)}).wait_recv()
@@ -310,7 +321,7 @@
             jax.ShapeDtypeStruct((own_rows, depth), bf16),
             jax.ShapeDtypeStruct(scales.shape, jnp.float32),
         ),
-        in_specs=[vmem, hbm, hbm, vmem, pl.BlockSpec(memory_space=pltpu.SMEM)],
+        in_specs=[vmem, hbm, hbm, vmem, vmem],
         out_specs=(vmem, vmem),
         scratch_shapes=[
             pltpu.VMEM((chunks, 2, depth, FC), bf16),
@@ -327,6 +338,7 @@
             pltpu.VMEM((2, PAD, depth), bf16),
             pltpu.VMEM((4, PAD, depth), bf16),
             pltpu.VMEM((3, PAD, depth), bf16),
+            pltpu.VMEM(scales.shape, jnp.float32),
             dma((chunks,)), dma((2,)), dma((items,)), dma((items,)), dma((8,)), dma((8,)),
             dma((2,)), dma((2,)), dma((2,)), dma((2,)), dma((3,)), dma((3,)),
         ],

time: 102 us -> 99.6 us (0.976)
  Pallas kernels: 96.4 us -> 93.9 us
    pallas_call x1, Pallas kernels: 96.4 us -> 93.9 us  [fused(): pl.pallas_call(kernel, out_shape=(jax.ShapeDtypeStruct((own_rows, depth),...]
where the time goes in v2:
time: 99.6 us; the launch traced here: 99.4 us
  Pallas kernels  93.9 us (94%)
  local copies, waits for them, and re-layouts  4.77 us (5%)
    pallas_call x1, Pallas kernels, fused(): pl.pallas_call(kernel, out_shape=(jax.ShapeDtypeStruct((own_rows, depth),...  93.9 us
    unnamed x3, local copies, waits for them, and re-layouts  4.77 us

profile of v2, /device:TPU:0, one launch (start us, length us, event | category | flops | bytes accessed | tf_op | source)
XLA Modules:
  0.0 99.4 jit_solution(8732791521644722750)
XLA Ops:
  0.6 1.4 %copy.7.pattern_ref = s32[28,16]{1,0:T(8,128)} copy(s32[28,16]{0,1:T(8,128)} %param.9) | data formatting | bytes 3584 | tf_op args[4]
  2.0 93.9 %shard_map.68 = (bf16[28,2048]{1,0:T(8,128)(2,1)}, f32[2,16,3584]{2,1,0:T(8,128)}) custom-call(bf16[28,2048]{1,0:T(8,128)(2,1)} %tokens_ref.1, bf16[224,3584]{1,0:T(8,128)(2,1)} %hidden_ref.1, bf16[2,2048,3584]{2,1,0:T(8,128)(2,1)} %codes_ref.1, f32[2,16,3584]{2,1,0:T(8,128)} %scales_ref.1, s32[28,16]{1,0:T(8,128)} %copy.7.pattern_ref), custom_call_target="tpu_custom_call" | custom-call | flops 19730006016 | bytes 29360128 | tf_op jit(solution)/shard_map/pallas_call | solution.py:318
  96.0 1.6 %copy.10 = bf16[28,2048]{1,0:T(8,128)(2,1)} copy(bf16[28,2048]{1,0:T(8,128)(2,1)} %get-tuple-element.4) | data formatting | bytes 229376
  97.5 1.8 %copy.11 = f32[2,16,3584]{2,1,0:T(8,128)} copy(f32[2,16,3584]{2,1,0:T(8,128)} %get-tuple-element.5) | data formatting | bytes 917504
